TPU v7x, 256 devices: a whole 4x4x8 slice. The times are simulated.
256 devices in a mesh: seq: 64 (over z, x, core), head: 4 (over y).
Axes of the slice: x: 4, y: 4, z: 8, core: 2. Of those that a mesh axis runs over, the one named last changes fastest.
Arguments:
- query_key: bfloat16 [32768, 128], P('seq'), may hold values from -1.5 to 1.5
- values: bfloat16 [32768, 5120], P('seq', 'head'), may hold values from -0.119628906 to 0.119628906
- cotangent: bfloat16 [32768, 5120], P('seq', 'head'), may hold values from -0.119628906 to 0.119628906
- level_gain: float32 [16, 15, 80], P(None, None, 'head'), may hold values from 0.1 to 1
- level_code: int32 [512], P('seq'), may hold values from 0 to 15
Outputs:
- mixed: bfloat16 [32768, 5120], P('seq', 'head')
- grad_qk: float32 [32768, 128], P('seq')
- grad_values: bfloat16 [32768, 5120], P('seq', 'head')
Inputs may be any that keep to these rules, and one draw needn't show every extreme that they name: `level_code`: each span's row of the weight table.
All inputs are finite; a program needn't handle non-finite values.
Results may differ from a plain program's by a relative error of at most 0.005.
Values sent between devices are 32-bit elements; how exact they have to be, the bound alone decides.
No kernel may reach another device: no remote copies, remote signals or barrier semaphores. Data moves between devices by JAX's collectives and lax.ppermute only.
A program may use at most 128 MiB of HBM per device.

v0:
```python
import jax
import jax.numpy as jnp
from jax import lax
from jax.sharding import PartitionSpec as P

HEAD_DIM = 64
CH = 64
precise = lax.Precision.HIGHEST


def partner_2(value, axis, bit):
    mask = 2**bit
    pairs = [(source, source ^ mask) for source in range(lax.axis_size(axis))]
    return lax.ppermute(value, axis, pairs)


def bit_length(numbers, top_bits):
    bit_total = jnp.zeros_like(numbers)
    for bit_power in range(top_bits):
        bit_total = bit_total + (numbers >= 1 << bit_power).astype(jnp.int32)
    return bit_total


def local_levels(span_count):
    span_ids = jnp.arange(span_count, dtype=jnp.int32)
    return bit_length(span_ids[:, None] ^ span_ids[None, :], 8)


def local(query_key, values, cotangent, level_gain, level_code):
    tok_rows, state_dim = query_key.shape
    head_cols = values.shape[1]
    codes, levels, group_heads = level_gain.shape
    span_count = tok_rows // CH
    span_levels = span_count.bit_length() - 1
    seq_levels = lax.axis_size("seq").bit_length() - 1
    position = lax.axis_index("seq")
    picked = (level_code[:, None] == jnp.arange(codes, dtype=jnp.int32)[None, :]).astype(
        jnp.float32
    )
    level_weight = jnp.dot(
        picked, level_gain.reshape(codes, levels * group_heads), precision=precise
    ).reshape(span_count, levels, group_heads)
    cross_cols = jnp.repeat(
        level_weight[:, span_levels + 1 : span_levels + 1 + seq_levels, :], HEAD_DIM, axis=-1
    )
    own_state = lax.dot_general(
        query_key, values, (((0,), (0,)), ((), ())), preferred_element_type=jnp.float32
    )
    q_spans = query_key.reshape(span_count, CH, state_dim)
    c_spans = cotangent.reshape(span_count, CH, head_cols)
    span_grad = jnp.einsum("cti,ctj->cij", q_spans, c_spans, preferred_element_type=jnp.float32)
    level_grad = jnp.einsum("cij,clj->lij", span_grad, cross_cols, precision=precise)
    siblings = []
    adjoint = jnp.zeros_like(own_state)
    block_sum = own_state
    level_carry = level_grad
    for level_bit in range(seq_levels):
        partner = partner_2(block_sum, "seq", level_bit)
        upper_half = position >> level_bit & 1 == 1
        siblings.append(jnp.where(upper_half, partner, 0.0))
        block_sum = block_sum + partner
    for level_bit in range(seq_levels):
        partner_grad = partner_2(level_carry, "seq", level_bit)
        upper_half = position >> level_bit & 1 == 1
        adjoint = adjoint + jnp.where(upper_half, 0.0, partner_grad[0])
        level_carry = (level_carry + partner_grad)[1:]
    sibling = jnp.stack(siblings)
    span_state = jnp.einsum("clj,lij->cij", cross_cols, sibling, precision=precise).astype(
        jnp.bfloat16
    )
    adjoint_bf = adjoint.astype(jnp.bfloat16)
    scores = lax.dot_general(
        query_key, query_key, (((1,), (1,)), ((), ())), preferred_element_type=jnp.float32
    )
    onehot = (
        local_levels(span_count)[:, :, None]
        == jnp.arange(span_levels + 1, dtype=jnp.int32)[None, None, :]
    ).astype(jnp.float32)
    local_weight = jnp.einsum(
        "abk,akg->gab", onehot, level_weight[:, : span_levels + 1, :], precision=precise
    )
    causal = jnp.tril(jnp.ones((tok_rows, tok_rows), dtype=bool))
    pair_cols = 2 * HEAD_DIM

    def head_pair(pair_index, running):
        inner_out, dv_inner, d_score = running
        col_start = pair_index * pair_cols
        val_pair = lax.dynamic_slice_in_dim(values, col_start, pair_cols, 1).reshape(
            tok_rows, 2, HEAD_DIM
        )
        cot_pair = lax.dynamic_slice_in_dim(cotangent, col_start, pair_cols, 1).reshape(
            tok_rows, 2, HEAD_DIM
        )
        pair_weight = lax.dynamic_slice_in_dim(local_weight, pair_index * 2, 2, 0)
        weight = jnp.broadcast_to(
            pair_weight[:, :, None, :, None], (2, span_count, CH, span_count, CH)
        ).reshape(2, tok_rows, tok_rows)
        mixing = jnp.where(causal, weight * scores, 0.0).astype(jnp.bfloat16)
        part_out = jnp.einsum(
            "gts,sgp->tgp", mixing, val_pair, preferred_element_type=jnp.float32
        ).reshape(tok_rows, pair_cols)
        d_mix = jnp.einsum("tgp,sgp->gts", cot_pair, val_pair, preferred_element_type=jnp.float32)
        d_score = d_score + jnp.sum(jnp.where(causal, weight * d_mix, 0.0), axis=0)
        part_dv = jnp.einsum(
            "gts,tgp->sgp", mixing, cot_pair, preferred_element_type=jnp.float32
        ).reshape(tok_rows, pair_cols)
        inner_out = lax.dynamic_update_slice_in_dim(inner_out, part_out, col_start, 1)
        dv_inner = lax.dynamic_update_slice_in_dim(dv_inner, part_dv, col_start, 1)
        return (inner_out, dv_inner, d_score)

    start_state = (
        jnp.zeros((tok_rows, head_cols), jnp.float32),
        jnp.zeros((tok_rows, head_cols), jnp.float32),
        jnp.zeros((tok_rows, tok_rows), jnp.float32),
    )
    inner_out, dv_inner, d_score = lax.fori_loop(0, group_heads // 2, head_pair, start_state)
    outer_out = jnp.einsum(
        "cti,cij->ctj", q_spans, span_state, preferred_element_type=jnp.float32
    ).reshape(tok_rows, head_cols)
    mixed = (inner_out + outer_out).astype(jnp.bfloat16)
    dq_outer = jnp.einsum(
        "ctj,cij->cti", c_spans, span_state, preferred_element_type=jnp.float32
    ).reshape(tok_rows, state_dim)
    dv_outer = jnp.dot(query_key, adjoint_bf, preferred_element_type=jnp.float32)
    dk_outer = lax.dot_general(
        values, adjoint_bf, (((1,), (1,)), ((), ())), preferred_element_type=jnp.float32
    )
    q_float = query_key.astype(jnp.float32)
    dq_inner = jnp.dot(d_score, q_float, precision=precise) + lax.dot_general(
        d_score, q_float, (((0,), (0,)), ((), ())), precision=precise
    )
    head_part = dq_inner + dq_outer + dk_outer
    grad_qk = lax.psum(head_part, "head")
    grad_values = (dv_inner + dv_outer).astype(jnp.bfloat16)
    return (mixed, grad_qk, grad_values)


def solution(mesh):
    placed = (P("seq", None), P("seq", "head"), P("seq", "head"), P(None, None, "head"), P("seq"))
    return jax.shard_map(
        local,
        mesh=mesh,
        in_specs=placed,
        out_specs=(P("seq", "head"), P("seq", None), P("seq", "head")),
        check_vma=False,
    )
```

profile of v0, /device:TPU:2, one launch (start us, length us, event | category | flops | bytes accessed | tf_op | source)
XLA Modules:
  0.0 713.1 jit_solution(9387156875039487626)
XLA Ops:
  8.1 4.5 fusion.36
  12.6 6.3 copy.78
  24.0 10.4 %fusion.37 = f32[1280,6,128]{2,1,0:T(8,128)} fusion(f32[8,6,1280]{0,1,2:T(8,128)S(1)} %bitcast.108, f32[8,128,1280]{1,0,2:T(8,128)S(1)} %copy-done.4), kind=kOutput, calls=%fused_computation.70 | convolution fusion | flops 94371840 | bytes 9420800 | tf_op jit(solution)/shard_map/cij,clj->lij/dot_general | solution.py:52
  34.4 5.7 copy.79
  40.0 7.0 collective-permute-done.6
  47.0 3.8 slice_add_fusion
  53.2 71.2 %collective-permute-done.7 = f32[5,128,1280]{2,1,0:T(8,128)S(1)} collective-permute-done((f32[5,128,1280]{2,1,0:T(8,128)S(1)}, f32[5,128,1280]{2,1,0:T(8,128)S(1)}, u32[]{:S(2)}, u32[]{:S(2)}) %collective-permute-start.7) | collective-permute-done | bytes 3276832 | tf_op jit(solution)/shard_map/ppermute | solution.py:14
  135.8 64.5 %collective-permute-done.1 = f32[128,1280]{1,0:T(8,128)S(1)} collective-permute-done((f32[128,1280]{1,0:T(8,128)S(1)}, f32[128,1280]{1,0:T(8,128)S(1)}, u32[]{:S(2)}, u32[]{:S(2)}) %collective-permute-start.1) | collective-permute-done | bytes 655392 | tf_op jit(solution)/shard_map/ppermute | solution.py:14
  202.9 3.7 slice_add_fusion.2
  210.4 230.9 %while.19 = (s32[]{:T(128)}, f32[512,1280]{1,0:T(8,128)}, f32[512,1280]{0,1:T(8,128)}, f32[512,512]{1,0:T(8,128)}, bf16[512,1280]{1,0:T(8,128)(2,1)S(1)}, /*inde...) while((s32[]{:T(128)}, f32[512,1280]{1,0:T(8,128)}, ...), condition=%wide.region_2.3_spmd.clone.clone, body=%wide.region_0.2_spmd.clone.clone.sunk | while | flops 204996608 | bytes 29099832 | solution.py:116
  215.8 3.4 reshape.141
  238.0 3.4 reshape.141
  261.2 3.4 reshape.141
  284.4 3.4 reshape.141
  400.3 3.4 reshape.141
  450.9 21.2 %collective-permute-done.3 = f32[128,1280]{1,0:T(8,128)S(1)} collective-permute-done((f32[128,1280]{1,0:T(8,128)S(1)}, f32[128,1280]{1,0:T(8,128)S(1)}, u32[]{:S(2)}, u32[]{:S(2)}) %collective-permute-start.3) | collective-permute-done | bytes 655392 | tf_op jit(solution)/shard_map/ppermute | solution.py:14
  474.1 59.5 %collective-permute-done.4 = f32[128,1280]{1,0:T(8,128)S(1)} collective-permute-done((f32[128,1280]{1,0:T(8,128)S(1)}, f32[128,1280]{1,0:T(8,128)S(1)}, u32[]{:S(2)}, u32[]{:S(2)}) %collective-permute-start.4) | collective-permute-done | bytes 655392 | tf_op jit(solution)/shard_map/ppermute | solution.py:14
  533.7 6.0 collective-permute-start.5
  541.9 34.5 %collective-permute-done.5 = f32[128,1280]{1,0:T(8,128)S(1)} collective-permute-done((f32[128,1280]{1,0:T(8,128)S(1)}, f32[128,1280]{1,0:T(8,128)S(1)}, u32[]{:S(2)}, u32[]{:S(2)}) %collective-permute-start.5) | collective-permute-done | bytes 655392 | tf_op jit(solution)/shard_map/ppermute | solution.py:14
  576.5 17.7 %collective-permute-done.11 = f32[1,128,1280]{2,1,0:T(8,128)S(1)} collective-permute-done((f32[1,128,1280]{2,1,0:T(8,128)S(1)}, f32[1,128,1280]{2,1,0:T(8,128)S(1)}, u32[]{:S(2)}, u32[]{:S(2)}) %collective-permute-start.11) | collective-permute-done | bytes 655392 | tf_op jit(solution)/shard_map/ppermute | solution.py:14
  597.2 5.7 copy.73
  602.9 13.7 %convert_bitcast_fusion = bf16[8,128,1280]{1,0,2:T(8,128)(2,1)} fusion(f32[6,128,1280]{1,0,2:T(8,128)} %copy.73, f32[8,6,1280]{0,1,2:T(8,128)} %bitcast.109), kind=kOutput, calls=%fused_computation.17 | convolution fusion | flops 95682560 | bytes 6799360 | tf_op jit(solution)/shard_map/clj,lij->cij/dot_general | solution.py:68
  616.6 3.8 copy.75
  632.3 72.3 %all-reduce.2.cloned.1.call-done = f32[512,128]{1,0:T(8,128)} async-done(((f32[512,128]{1,0:T(8,128)}), f32[512,128]{1,0:T(8,128)}) %all-reduce.2.cloned.1.call-update) | async-done | bytes 262160 | tf_op jit(solution)/shard_map/psum | solution.py:133
  (274 shorter events, 269.4 us)
Async XLA Ops:
  7.2 697.4 %all-reduce.2.cloned.1.call-start = ((), (), s32[]{:S(2)}) async-start(), calls=%async_computation | async-start | bytes 524288 | tf_op jit(solution)/shard_map/psum | solution.py:133
  12.6 6.3 copy-start.16
  12.6 6.6 copy-start.17
  19.6 4.4 copy-start.4
  19.9 2.7 copy-start.2
  40.0 7.0 collective-permute-start.6
  47.0 3.8 copy-start.10
  50.8 77.7 %copy-start.7 = (bf16[512,1280]{1,0:T(8,128)(2,1)S(1)}, bf16[512,1280]{1,0:T(8,128)(2,1)}, u32[]{:S(2)}) copy-start(bf16[512,1280]{1,0:T(8,128)(2,1)} %param.8) | copy-start | bytes 3932164
  50.8 73.6 %collective-permute-start.7 = (f32[5,128,1280]{2,1,0:T(8,128)S(1)}, f32[5,128,1280]{2,1,0:T(8,128)S(1)}, u32[]{:S(2)}, u32[]{:S(2)}) collective-permute-start(f32[5,128,1280]{2,1,0:T(8,128)S(1)} %slice_add_fusion), channel_id=1, source_target_pairs={{0,8},{4,12},{8,0},{12,4},{16,24},{20,28},{24,16},{28,20},{32,40},... | collective-permute-start | bytes 9830408 | tf_op jit(solution)/shard_map/ppermute | solution.py:14
  126.9 76.0 %collective-permute-start.8 = (f32[4,128,1280]{2,1,0:T(8,128)}, f32[4,128,1280]{2,1,0:T(8,128)}, u32[]{:S(2)}, u32[]{:S(2)}) collective-permute-start(f32[4,128,1280]{2,1,0:T(8,128)} %slice_add_fusion.1), channel_id=1, source_target_pairs={{0,16},{4,20},{8,24},{12,28},{16,0},{20,4},{24,8},{28,12},{32,48},... | collective-permute-start | bytes 7864328 | tf_op jit(solution)/shard_map/ppermute | solution.py:14
  128.9 2.2 collective-permute-start
  132.0 68.3 %collective-permute-start.1 = (f32[128,1280]{1,0:T(8,128)S(1)}, f32[128,1280]{1,0:T(8,128)S(1)}, u32[]{:S(2)}, u32[]{:S(2)}) collective-permute-start(f32[128,1280]{1,0:T(8,128)S(1)} %add.163), channel_id=1, source_target_pairs={{0,8},{4,12},{8,0},{12,4},{16,24},{20,28},{24,16},{28,20},{32,40},... | collective-permute-start | bytes 1966088 | tf_op jit(solution)/shard_map/ppermute | solution.py:14
  200.2 6.3 copy-start.12
  201.3 241.8 %collective-permute-start.2 = (f32[128,1280]{1,0:T(8,128)}, f32[128,1280]{1,0:T(8,128)}, u32[]{:S(2)}, u32[]{:S(2)}) collective-permute-start(f32[128,1280]{1,0:T(8,128)} %add.164), channel_id=1, source_target_pairs={{0,16},{4,20},{8,24},{12,28},{16,0},{20,4},{24,8},{28,12},{32,48},... | collective-permute-start | bytes 1966088 | tf_op jit(solution)/shard_map/ppermute | solution.py:14
  206.6 239.8 %collective-permute-start.9 = (f32[3,128,1280]{2,1,0:T(8,128)}, f32[3,128,1280]{2,1,0:T(8,128)}, u32[]{:S(2)}, u32[]{:S(2)}) collective-permute-start(f32[3,128,1280]{2,1,0:T(8,128)} %slice_add_fusion.2), channel_id=1, source_target_pairs={{0,32},{4,36},{8,40},{12,44},{16,48},{20,52},{24,56},{28,60},{32,0... | collective-permute-start | bytes 5898248 | tf_op jit(solution)/shard_map/ppermute | solution.py:14
  443.1 6.9 copy-start.15
  444.5 27.6 %collective-permute-start.3 = (f32[128,1280]{1,0:T(8,128)S(1)}, f32[128,1280]{1,0:T(8,128)S(1)}, u32[]{:S(2)}, u32[]{:S(2)}) collective-permute-start(f32[128,1280]{1,0:T(8,128)S(1)} %add.165), channel_id=1, source_target_pairs={{0,32},{4,36},{8,40},{12,44},{16,48},{20,52},{24,56},{28,60},{32,0... | collective-permute-start | bytes 1966088 | tf_op jit(solution)/shard_map/ppermute | solution.py:14
  448.2 24.1 %copy-start.13 = (f32[128,1280]{1,0:T(8,128)S(1)}, f32[128,1280]{1,0:T(8,128)}, u32[]{:S(2)}) copy-start(f32[128,1280]{1,0:T(8,128)} %copy-done.12) | copy-start | bytes 1966084
  448.2 91.6 %collective-permute-start.10 = (f32[2,128,1280]{2,1,0:T(8,128)S(1)}, f32[2,128,1280]{2,1,0:T(8,128)S(1)}, u32[]{:S(2)}, u32[]{:S(2)}) collective-permute-start(f32[2,128,1280]{2,1,0:T(8,128)S(1)} %slice_add_fusion.3), channel_id=1, source_target_pairs={{0,64},{4,68},{8,72},{12,76},{16,80},{20,84},{24,88},{28,92},{32,9... | collective-permute-start | bytes 3932168 | tf_op jit(solution)/shard_map/ppermute | solution.py:14
  472.2 61.5 %collective-permute-start.4 = (f32[128,1280]{1,0:T(8,128)S(1)}, f32[128,1280]{1,0:T(8,128)S(1)}, u32[]{:S(2)}, u32[]{:S(2)}) collective-permute-start(f32[128,1280]{1,0:T(8,128)S(1)} %add.166), channel_id=1, source_target_pairs={{0,64},{4,68},{8,72},{12,76},{16,80},{20,84},{24,88},{28,92},{32,9... | collective-permute-start | bytes 1966088 | tf_op jit(solution)/shard_map/ppermute | solution.py:14
  533.7 42.7 %collective-permute-start.5 = (f32[128,1280]{1,0:T(8,128)S(1)}, f32[128,1280]{1,0:T(8,128)S(1)}, u32[]{:S(2)}, u32[]{:S(2)}) collective-permute-start(f32[128,1280]{1,0:T(8,128)S(1)} %add.167), channel_id=1, source_target_pairs={{0,128},{4,132},{8,136},{12,140},{16,144},{20,148},{24,152},{28,15... | collective-permute-start | bytes 1966088 | tf_op jit(solution)/shard_map/ppermute | solution.py:14
  539.9 54.4 %collective-permute-start.11 = (f32[1,128,1280]{2,1,0:T(8,128)S(1)}, f32[1,128,1280]{2,1,0:T(8,128)S(1)}, u32[]{:S(2)}, u32[]{:S(2)}) collective-permute-start(f32[1,128,1280]{2,1,0:T(8,128)S(1)} %slice_add_fusion.4), channel_id=1, source_target_pairs={{0,128},{4,132},{8,136},{12,140},{16,144},{20,148},{24,152},{28,15... | collective-permute-start | bytes 1966088 | tf_op jit(solution)/shard_map/ppermute | solution.py:14
  622.8 3.0 copy-start.9
  627.0 3.2 copy-start.6
  (25 other events, 51.0 us)
Sparse Core Ops, SparseCore 0:
  627.1 77.3 all-reduce.1
where the time goes:
time: 717 us; the launch traced here: 713 us
  waiting for transfers between devices  350 us (49%)
  local copies, waits for them, and re-layouts  184 us (26%)
  matrix products  80 us (11%)
  other arithmetic  66.8 us (9%)
  starting transfers between devices  17.5 us (2%)
  between operations  14.3 us (2%)
    ppermute x12, waiting for transfers between devices, partner_2(): return lax.ppermute(value, axis, pairs)  278 us
    psum x1, waiting for transfers between devices, local(): grad_qk = lax.psum(head_part, 'head')  72.3 us
    dynamic_update_slice x20, local copies, waits for them, and re-layouts, head_pair(): lax.dynamic_update_slice_in_dim(inner_out, part_out, col_start, 1)  35 us
    reshape x10, local copies, waits for them, and re-layouts, head_pair(): weight = jnp.broadcast_to(pair_weight[:, :, None, :, None], (2, span_coun...  34.2 us
    dynamic_slice x20, local copies, waits for them, and re-layouts, head_pair(): lax.dynamic_slice_in_dim(cotangent, col_start, pair_cols, 1)  32.4 us
    broadcast_in_dim x10, local copies, waits for them, and re-layouts, head_pair(): jnp.broadcast_to(pair_weight[:, :, None, :, None], (2, span_count, CH, sp...  24 us
    add x10, other arithmetic, head_pair(): d_score = d_score + jnp.sum(jnp.where(causal, weight * d_mix, 0.0), axis=0)  23.9 us
    ppermute x12, starting transfers between devices, partner_2(): return lax.ppermute(value, axis, pairs)  17.5 us
  transfers between devices with their start and end apart: 13, of which 9 were waited for; matrix products, arithmetic and copies ran while one was open for 36% of the time, Pallas kernels for 0%

commit v1 on v0

--- a/solution.py
+++ b/solution.py
@@ -130,7 +130,11 @@
         d_score, q_float, (((0,), (0,)), ((), ())), precision=precise
     )
     head_part = dq_inner + dq_outer + dk_outer
-    grad_qk = lax.psum(head_part, "head")
+    size = lax.axis_size("head")
+    grad_qk, far = (head_part, 1)
+    while far < size:
+        grad_qk = grad_qk + lax.ppermute(grad_qk, "head", [(i, i ^ far) for i in range(size)])
+        far = 2 * far
     grad_values = (dv_inner + dv_outer).astype(jnp.bfloat16)
     return (mixed, grad_qk, grad_values)
 

time: 717 us -> 669 us (0.933)
  the two profiles are of different devices: /device:TPU:2 before, /device:TPU:120 now
where the time goes in v1:
time: 669 us; the launch traced here: 665 us
  waiting for transfers between devices  261 us (39%)
  local copies, waits for them, and re-layouts  183 us (27%)
  matrix products  77.7 us (12%)
  starting transfers between devices  76.7 us (11%)
  other arithmetic  65.8 us (10%)
    ppermute x12, waiting for transfers between devices, partner_2(): return lax.ppermute(value, axis, pairs)  252 us
    ppermute x12, starting transfers between devices, partner_2(): return lax.ppermute(value, axis, pairs)  74.6 us
    dynamic_update_slice x20, local copies, waits for them, and re-layouts, head_pair(): lax.dynamic_update_slice_in_dim(inner_out, part_out, col_start, 1)  35.1 us
    reshape x10, local copies, waits for them, and re-layouts, head_pair(): weight = jnp.broadcast_to(pair_weight[:, :, None, :, None], (2, span_coun...  34.2 us
    dynamic_slice x20, local copies, waits for them, and re-layouts, head_pair(): lax.dynamic_slice_in_dim(cotangent, col_start, pair_cols, 1)  32.4 us
    add x10, other arithmetic, head_pair(): d_score = d_score + jnp.sum(jnp.where(causal, weight * d_mix, 0.0), axis=0)  23.9 us
    broadcast_in_dim x10, local copies, waits for them, and re-layouts, head_pair(): jnp.broadcast_to(pair_weight[:, :, None, :, None], (2, span_count, CH, sp...  23.9 us
    dot_general x10, matrix products, head_pair(): jnp.einsum('tgp,sgp->gts', cot_pair, val_pair, preferred_element_type=jnp...  17 us
  transfers between devices with their start and end apart: 14, of which 10 were waited for; matrix products, arithmetic and copies ran while one was open for 38% of the time, Pallas kernels for 0%

profile of v1, /device:TPU:120, one launch (start us, length us, event | category | flops | bytes accessed | tf_op | source)
XLA Modules:
  0.0 665.3 jit_solution(14044279545544186264)
XLA Ops:
  1.5 4.5 fusion.36
  6.1 6.3 copy.78
  17.4 10.3 %fusion.37 = f32[1280,6,128]{2,1,0:T(8,128)} fusion(f32[8,6,1280]{0,1,2:T(8,128)S(1)} %bitcast.108, f32[8,128,1280]{1,0,2:T(8,128)S(1)} %copy-done.4), kind=kOutput, calls=%fused_computation.70 | convolution fusion | flops 94371840 | bytes 9420800 | tf_op jit(solution)/shard_map/cij,clj->lij/dot_general | solution.py:52
  27.7 5.7 copy.79
  33.4 7.0 %collective-permute-done.6 = f32[6,128,1280]{2,1,0:T(8,128)S(1)} collective-permute-done((f32[6,128,1280]{2,1,0:T(8,128)}, f32[6,128,1280]{2,1,0:T(8,128)S(1)}, u32[]{:S(2)}, u32[]{:S(2)}) %collective-permute-start.6) | collective-permute-done | bytes 3932192 | tf_op jit(solution)/shard_map/ppermute | solution.py:14
  40.4 3.8 slice_add_fusion
  45.8 71.5 %collective-permute-done.7 = f32[5,128,1280]{2,1,0:T(8,128)S(1)} collective-permute-done((f32[5,128,1280]{2,1,0:T(8,128)S(1)}, f32[5,128,1280]{2,1,0:T(8,128)S(1)}, u32[]{:S(2)}, u32[]{:S(2)}) %collective-permute-start.7) | collective-permute-done | bytes 3276832 | tf_op jit(solution)/shard_map/ppermute | solution.py:14
  129.2 64.5 %collective-permute-done.1 = f32[128,1280]{1,0:T(8,128)S(1)} collective-permute-done((f32[128,1280]{1,0:T(8,128)S(1)}, f32[128,1280]{1,0:T(8,128)S(1)}, u32[]{:S(2)}, u32[]{:S(2)}) %collective-permute-start.1) | collective-permute-done | bytes 655392 | tf_op jit(solution)/shard_map/ppermute | solution.py:14
  196.8 3.7 slice_add_fusion.2
  204.1 231.0 %while.19 = (s32[]{:T(128)}, f32[512,1280]{1,0:T(8,128)}, f32[512,1280]{0,1:T(8,128)}, f32[512,512]{1,0:T(8,128)}, bf16[512,1280]{1,0:T(8,128)(2,1)S(1)}, /*inde...) while((s32[]{:T(128)}, f32[512,1280]{1,0:T(8,128)}, ...), condition=%wide.region_2.3_spmd.clone.clone, body=%wide.region_0.2_spmd.clone.clone.sunk | while | flops 204996608 | bytes 29099832 | solution.py:116
  209.5 3.4 reshape.141
  231.8 3.4 reshape.141
  255.0 3.4 reshape.141
  278.2 3.4 reshape.141
  443.2 18.7 %collective-permute-done.3 = f32[128,1280]{1,0:T(8,128)S(1)} collective-permute-done((f32[128,1280]{1,0:T(8,128)S(1)}, f32[128,1280]{1,0:T(8,128)S(1)}, u32[]{:S(2)}, u32[]{:S(2)}) %collective-permute-start.3) | collective-permute-done | bytes 655392 | tf_op jit(solution)/shard_map/ppermute | solution.py:14
  467.2 60.4 %collective-permute-done.4 = f32[128,1280]{1,0:T(8,128)S(1)} collective-permute-done((f32[128,1280]{1,0:T(8,128)S(1)}, f32[128,1280]{1,0:T(8,128)S(1)}, u32[]{:S(2)}, u32[]{:S(2)}) %collective-permute-start.4) | collective-permute-done | bytes 655392 | tf_op jit(solution)/shard_map/ppermute | solution.py:14
  527.7 61.3 %collective-permute-start.5 = (f32[128,1280]{1,0:T(8,128)S(1)}, f32[128,1280]{1,0:T(8,128)S(1)}, u32[]{:S(2)}, u32[]{:S(2)}) collective-permute-start(f32[128,1280]{1,0:T(8,128)S(1)} %add.171), channel_id=1, source_target_pairs={{0,128},{4,132},{8,136},{12,140},{16,144},{20,148},{24,152},{28,15... | collective-permute-start | bytes 1966088 | tf_op jit(solution)/shard_map/ppermute | solution.py:14
  591.1 13.0 %collective-permute-done.5 = f32[128,1280]{1,0:T(8,128)S(1)} collective-permute-done((f32[128,1280]{1,0:T(8,128)S(1)}, f32[128,1280]{1,0:T(8,128)S(1)}, u32[]{:S(2)}, u32[]{:S(2)}) %collective-permute-start.5) | collective-permute-done | bytes 655392 | tf_op jit(solution)/shard_map/ppermute | solution.py:14
  604.2 14.6 %collective-permute-done.11 = f32[1,128,1280]{2,1,0:T(8,128)S(1)} collective-permute-done((f32[1,128,1280]{2,1,0:T(8,128)S(1)}, f32[1,128,1280]{2,1,0:T(8,128)S(1)}, u32[]{:S(2)}, u32[]{:S(2)}) %collective-permute-start.11) | collective-permute-done | bytes 655392 | tf_op jit(solution)/shard_map/ppermute | solution.py:14
  621.8 5.8 copy.73
  627.5 13.7 %convert_bitcast_fusion = bf16[8,128,1280]{1,0,2:T(8,128)(2,1)} fusion(f32[6,128,1280]{1,0,2:T(8,128)} %copy.73, f32[8,6,1280]{0,1,2:T(8,128)} %bitcast.109), kind=kOutput, calls=%fused_computation.17 | convolution fusion | flops 95682560 | bytes 6799360 | tf_op jit(solution)/shard_map/clj,lij->cij/dot_general | solution.py:68
  641.2 3.8 copy.75
  652.4 4.2 collective-permute-done.12
  659.9 4.7 collective-permute-done.13
  (276 shorter events, 272.8 us)
Async XLA Ops:
  6.1 6.3 copy-start.16
  6.1 6.6 copy-start.17
  13.0 4.4 copy-start.4
  33.4 7.0 %collective-permute-start.6 = (f32[6,128,1280]{2,1,0:T(8,128)}, f32[6,128,1280]{2,1,0:T(8,128)S(1)}, u32[]{:S(2)}, u32[]{:S(2)}) collective-permute-start(f32[6,128,1280]{2,1,0:T(8,128)} %bitcast.116), channel_id=1, source_target_pairs={{0,4},{4,0},{8,12},{12,8},{16,20},{20,16},{24,28},{28,24},{32,36},... | collective-permute-start | bytes 11796488 | tf_op jit(solution)/shard_map/ppermute | solution.py:14
  40.4 3.8 copy-start.10
  44.2 78.6 %copy-start.7 = (bf16[512,1280]{1,0:T(8,128)(2,1)S(1)}, bf16[512,1280]{1,0:T(8,128)(2,1)}, u32[]{:S(2)}) copy-start(bf16[512,1280]{1,0:T(8,128)(2,1)} %param.8) | copy-start | bytes 3932164
  44.2 73.0 %collective-permute-start.7 = (f32[5,128,1280]{2,1,0:T(8,128)S(1)}, f32[5,128,1280]{2,1,0:T(8,128)S(1)}, u32[]{:S(2)}, u32[]{:S(2)}) collective-permute-start(f32[5,128,1280]{2,1,0:T(8,128)S(1)} %slice_add_fusion), channel_id=1, source_target_pairs={{0,8},{4,12},{8,0},{12,4},{16,24},{20,28},{24,16},{28,20},{32,40},... | collective-permute-start | bytes 9830408 | tf_op jit(solution)/shard_map/ppermute | solution.py:14
  119.8 77.0 %collective-permute-start.8 = (f32[4,128,1280]{2,1,0:T(8,128)}, f32[4,128,1280]{2,1,0:T(8,128)}, u32[]{:S(2)}, u32[]{:S(2)}) collective-permute-start(f32[4,128,1280]{2,1,0:T(8,128)} %slice_add_fusion.1), channel_id=1, source_target_pairs={{0,16},{4,20},{8,24},{12,28},{16,0},{20,4},{24,8},{28,12},{32,48},... | collective-permute-start | bytes 7864328 | tf_op jit(solution)/shard_map/ppermute | solution.py:14
  123.2 2.2 collective-permute-start
  126.3 67.4 %collective-permute-start.1 = (f32[128,1280]{1,0:T(8,128)S(1)}, f32[128,1280]{1,0:T(8,128)S(1)}, u32[]{:S(2)}, u32[]{:S(2)}) collective-permute-start(f32[128,1280]{1,0:T(8,128)S(1)} %add.167), channel_id=1, source_target_pairs={{0,8},{4,12},{8,0},{12,4},{16,24},{20,28},{24,16},{28,20},{32,40},... | collective-permute-start | bytes 1966088 | tf_op jit(solution)/shard_map/ppermute | solution.py:14
  193.7 6.8 %copy-start.12 = (f32[128,1280]{1,0:T(8,128)}, f32[128,1280]{1,0:T(8,128)S(1)}, u32[]{:S(2)}) copy-start(f32[128,1280]{1,0:T(8,128)S(1)} %collective-permute-done.1) | copy-start | bytes 1966084
  194.8 242.1 %collective-permute-start.2 = (f32[128,1280]{1,0:T(8,128)}, f32[128,1280]{1,0:T(8,128)}, u32[]{:S(2)}, u32[]{:S(2)}) collective-permute-start(f32[128,1280]{1,0:T(8,128)} %add.168), channel_id=1, source_target_pairs={{0,16},{4,20},{8,24},{12,28},{16,0},{20,4},{24,8},{28,12},{32,48},... | collective-permute-start | bytes 1966088 | tf_op jit(solution)/shard_map/ppermute | solution.py:14
  200.5 239.8 %collective-permute-start.9 = (f32[3,128,1280]{2,1,0:T(8,128)}, f32[3,128,1280]{2,1,0:T(8,128)}, u32[]{:S(2)}, u32[]{:S(2)}) collective-permute-start(f32[3,128,1280]{2,1,0:T(8,128)} %slice_add_fusion.2), channel_id=1, source_target_pairs={{0,32},{4,36},{8,40},{12,44},{16,48},{20,52},{24,56},{28,60},{32,0... | collective-permute-start | bytes 5898248 | tf_op jit(solution)/shard_map/ppermute | solution.py:14
  436.9 5.4 copy-start.15
  438.3 23.6 %collective-permute-start.3 = (f32[128,1280]{1,0:T(8,128)S(1)}, f32[128,1280]{1,0:T(8,128)S(1)}, u32[]{:S(2)}, u32[]{:S(2)}) collective-permute-start(f32[128,1280]{1,0:T(8,128)S(1)} %add.169), channel_id=1, source_target_pairs={{0,32},{4,36},{8,40},{12,44},{16,48},{20,52},{24,56},{28,60},{32,0... | collective-permute-start | bytes 1966088 | tf_op jit(solution)/shard_map/ppermute | solution.py:14
  442.2 23.2 %copy-start.13 = (f32[128,1280]{1,0:T(8,128)S(1)}, f32[128,1280]{1,0:T(8,128)}, u32[]{:S(2)}) copy-start(f32[128,1280]{1,0:T(8,128)} %copy-done.12) | copy-start | bytes 1966084
  442.2 146.8 %collective-permute-start.10 = (f32[2,128,1280]{2,1,0:T(8,128)S(1)}, f32[2,128,1280]{2,1,0:T(8,128)S(1)}, u32[]{:S(2)}, u32[]{:S(2)}) collective-permute-start(f32[2,128,1280]{2,1,0:T(8,128)S(1)} %slice_add_fusion.3), channel_id=1, source_target_pairs={{0,64},{4,68},{8,72},{12,76},{16,80},{20,84},{24,88},{28,92},{32,9... | collective-permute-start | bytes 3932168 | tf_op jit(solution)/shard_map/ppermute | solution.py:14
  462.0 65.6 %collective-permute-start.4 = (f32[128,1280]{1,0:T(8,128)S(1)}, f32[128,1280]{1,0:T(8,128)S(1)}, u32[]{:S(2)}, u32[]{:S(2)}) collective-permute-start(f32[128,1280]{1,0:T(8,128)S(1)} %add.170), channel_id=1, source_target_pairs={{0,64},{4,68},{8,72},{12,76},{16,80},{20,84},{24,88},{28,92},{32,9... | collective-permute-start | bytes 1966088 | tf_op jit(solution)/shard_map/ppermute | solution.py:14
  527.7 76.5 %collective-permute-start.5 = (f32[128,1280]{1,0:T(8,128)S(1)}, f32[128,1280]{1,0:T(8,128)S(1)}, u32[]{:S(2)}, u32[]{:S(2)}) collective-permute-start(f32[128,1280]{1,0:T(8,128)S(1)} %add.171), channel_id=1, source_target_pairs={{0,128},{4,132},{8,136},{12,140},{16,144},{20,148},{24,152},{28,15... | collective-permute-start | bytes 1966088 | tf_op jit(solution)/shard_map/ppermute | solution.py:14
  589.0 29.8 %collective-permute-start.11 = (f32[1,128,1280]{2,1,0:T(8,128)S(1)}, f32[1,128,1280]{2,1,0:T(8,128)S(1)}, u32[]{:S(2)}, u32[]{:S(2)}) collective-permute-start(f32[1,128,1280]{2,1,0:T(8,128)S(1)} %slice_add_fusion.4), channel_id=1, source_target_pairs={{0,128},{4,132},{8,136},{12,140},{16,144},{20,148},{24,152},{28,15... | collective-permute-start | bytes 1966088 | tf_op jit(solution)/shard_map/ppermute | solution.py:14
  647.9 3.0 copy-start.5
  650.1 6.5 collective-permute-start.12
  650.9 7.0 %copy-start.6 = (f32[512,1280]{0,1:T(8,128)S(1)}, f32[512,1280]{0,1:T(8,128)}, u32[]{:S(2)}) copy-start(f32[512,1280]{0,1:T(8,128)} %get-tuple-element.380) | copy-start | bytes 7864324
  656.6 8.0 %collective-permute-start.13 = (f32[512,128]{1,0:T(8,128)S(1)}, f32[512,128]{1,0:T(8,128)S(1)}, u32[]{:S(2)}, u32[]{:S(2)}) collective-permute-start(f32[512,128]{1,0:T(8,128)S(1)} %add.187), channel_id=1, source_target_pairs={{0,2},{1,3},{2,0},{3,1},{4,6},{5,7},{6,4},{7,5},{8,10},{9,11},{10,... | collective-permute-start | bytes 786440 | tf_op jit(solution)/shard_map/ppermute | solution.py:136
  (26 other events, 52.9 us)
